TPU v7x, 128 devices: a whole 4x4x4 slice. The times are simulated.
128 devices in a mesh: segment: 8 (over x, core), dp: 16 (over z, y).
Axes of the slice: x: 4, y: 4, z: 4, core: 2. Of those that a mesh axis runs over, the one named last changes fastest.
Arguments:
- embeds: bfloat16 [2, 16, 128, 4096], P(None, 'dp'), may hold values from -6 to 6
- base_weight: bfloat16 [8, 4096, 4096], P('segment', 'dp'), may hold values from -0.09375 to 0.09375
- norm_gain: float32 [8, 4096], P('segment'), may hold values from 0.25 to 1.75
- skill_down: bfloat16 [8, 16, 8, 4096], P('segment'), may hold values from -0.09375 to 0.09375
- skill_up: bfloat16 [8, 16, 8, 4096], P('segment'), may hold values from -2 to 2
- task_ids: int32 [2, 16], replicated, may hold values from 0 to 1835
- allocation: int32 [1836, 16], replicated, may hold values 0 or 1
- target_lengths: int32 [2, 16], replicated, may hold values from 1 to 128
- cotangent: bfloat16 [2, 16, 128, 4096], P(None, 'dp'), may hold values from -6 to 6
Outputs:
- hidden: bfloat16 [8, 2, 16, 128, 4096], P('segment', None, 'dp')
- input_grads: bfloat16 [8, 2, 16, 128, 4096], P('segment', None, 'dp')
- grad_down: float32 [8, 16, 8, 4096], P('segment', None, None, 'dp')
- grad_up: float32 [8, 16, 8, 4096], P('segment', None, None, 'dp')
All inputs are finite; a program needn't handle non-finite values.
Results may differ from a plain program's by a relative error of at most 0.019.
Values may be sent and summed in bfloat16 or wider, within the bound.
A program may use at most 192 MiB of HBM per device.

v0:
```python
import jax
import jax.numpy as jnp
from jax import lax
from jax.sharding import PartitionSpec as P

EPS = 1e-06


def shifted(block, axis, distance):
    devices = range(lax.axis_size(axis))
    route = [(i - distance, i) for i in devices if i - distance in devices]
    return lax.ppermute(block, axis, route)


def in_blocks(x, dim, size):
    before, after = (x.shape[:dim], x.shape[dim + 1 :])
    return jnp.moveaxis(x.reshape(*before, size, -1, *after), dim, 0)


def sent_and_summed(x, axis, dim):
    size = lax.axis_size(axis)
    parts = lax.all_to_all(in_blocks(x, dim, size), axis, 0, 0, tiled=True)
    return jnp.sum(parts.astype(jnp.float32), axis=0)


def side_by_side(arrays, axis, dim, along):
    both = jnp.concatenate(arrays, axis=along)
    result, at, done = (sent_and_summed(both, axis, dim), 0, [])
    for a in arrays:
        done.append(lax.slice_in_dim(result, at, at + a.shape[along], axis=along))
        at += a.shape[along]
    return tuple(done)


def prepare(x, gain, down_t):
    xf = x.astype(jnp.float32)
    inv = lax.rsqrt(jnp.mean(xf * xf, axis=-1, keepdims=True) + EPS)
    normed = (xf * inv * gain).astype(jnp.bfloat16)
    low = jnp.dot(normed, down_t.T, preferred_element_type=jnp.float32).astype(jnp.bfloat16)
    return (normed, low, inv)


def forward_full(x, weight, gain, down_t, up_t):
    normed, low, inv = prepare(x, gain, down_t)
    total = x.astype(jnp.float32) + jnp.dot(normed, weight, preferred_element_type=jnp.float32)
    total = total + jnp.dot(low, up_t, preferred_element_type=jnp.float32)
    return (total.astype(jnp.bfloat16), normed, low, inv)


def backward_core(x, normed, low, inv, grad_out, weight, gain, down_t, up_t):
    g_low = jnp.dot(grad_out, up_t.T, preferred_element_type=jnp.float32).astype(jnp.bfloat16)
    dnorm = jnp.dot(grad_out, weight.T, preferred_element_type=jnp.float32)
    dnorm = dnorm + jnp.dot(g_low, down_t, preferred_element_type=jnp.float32)
    seq_down = jnp.dot(g_low.T, normed, preferred_element_type=jnp.float32)
    seq_up = jnp.dot(low.T, grad_out, preferred_element_type=jnp.float32)
    xf = x.astype(jnp.float32)
    scaled = gain * dnorm
    grad_in = (
        grad_out.astype(jnp.float32)
        + inv * scaled
        - xf * inv * inv * inv * jnp.mean(xf * scaled, axis=-1, keepdims=True)
    )
    return (grad_in.astype(jnp.bfloat16), seq_down, seq_up)


def pick(table, index):
    return lax.dynamic_index_in_dim(table, index, 0, keepdims=False)


def place(table, value, index, active):
    return jnp.where(active, lax.dynamic_update_index_in_dim(table, value, index, 0), table)


def shards(
    embeds,
    base_weight,
    norm_gain,
    skill_down,
    skill_up,
    task_ids,
    allocation,
    target_lengths,
    cotangent,
):
    segments = lax.axis_size("segment")
    segment = lax.axis_index("segment")
    member = lax.axis_index("dp")
    weight = lax.all_gather(base_weight[0], "dp", axis=0, tiled=True)
    gain = norm_gain[0]
    micro = embeds.shape[0]
    rows = embeds.shape[2]
    width = embeds.shape[3]
    splits = 1
    blocks = micro * splits
    block_rows = rows // splits
    tasks = lax.dynamic_index_in_dim(task_ids, member, 1, keepdims=False)
    lengths = lax.dynamic_index_in_dim(target_lengths, member, 1, keepdims=False)
    onehot = (tasks[:, None] == jnp.arange(allocation.shape[0], dtype=jnp.int32)[None, :]).astype(
        jnp.float32
    )
    alloc = allocation.astype(jnp.float32)
    counts = jnp.maximum(jnp.sum(alloc, axis=1, keepdims=True), 1.0)
    mix = jnp.einsum("mt,ts->ms", onehot, alloc / counts, precision=lax.Precision.HIGHEST)
    down_seq = jnp.einsum(
        "ms,srd->mrd", mix, skill_down[0].astype(jnp.float32), precision=lax.Precision.HIGHEST
    ).astype(jnp.bfloat16)
    up_seq = jnp.einsum(
        "ms,srd->mrd", mix, skill_up[0].astype(jnp.float32), precision=lax.Precision.HIGHEST
    ).astype(jnp.bfloat16)
    down_all = jnp.repeat(down_seq, splits, axis=0)
    up_all = jnp.repeat(up_seq, splits, axis=0)
    mix_all = jnp.repeat(mix, splits, axis=0)
    firsts = embeds[:, 0]
    live = jnp.arange(rows, dtype=jnp.int32)[None, :] < lengths[:, None]
    seeds = cotangent[:, 0] * live[..., None].astype(jnp.bfloat16)
    ticks = segments + blocks - 1
    rank = down_all.shape[1]
    blank = jnp.zeros((block_rows, width), jnp.bfloat16)
    stack_blank = jnp.zeros((blocks, block_rows, width), jnp.bfloat16)
    low_blank = jnp.zeros((blocks, block_rows, rank), jnp.bfloat16)
    inv_blank = jnp.zeros((blocks, block_rows, 1), jnp.float32)

    def forward_tick(tick, carry):
        incoming, saved, outs, kept_norm, kept_low, kept_inv = carry
        slot = tick - segment
        active = (slot >= 0) & (slot < blocks)
        index = jnp.clip(slot, 0, blocks - 1)
        x = jnp.where(segment == 0, pick(firsts, index), incoming)
        result, normed, low, inv = lax.cond(
            active,
            lambda: forward_full(x, weight, gain, pick(down_all, index), pick(up_all, index)),
            lambda: (
                blank,
                blank,
                jnp.zeros((block_rows, rank), jnp.bfloat16),
                jnp.zeros((block_rows, 1), jnp.float32),
            ),
        )
        saved = place(saved, x, index, active)
        outs = place(outs, result, index, active)
        return (result, (saved, outs, kept_norm, kept_low, kept_inv))

    def forward_step(tick, carry):
        result, rest = forward_tick(tick, carry)
        moved = shifted(result, "segment", 1)
        return (moved,) + rest

    carry = (blank, stack_blank, stack_blank, stack_blank, low_blank, inv_blank)
    carry = lax.fori_loop(0, ticks - 1, forward_step, carry)
    _, (saved, outs, kept_norm, kept_low, kept_inv) = forward_tick(ticks - 1, carry)
    skills = skill_down.shape[1]
    acc_blank = jnp.zeros((skills, rank, width), jnp.float32)

    def backward_tick(tick, carry):
        incoming, grads_in, acc_down, acc_up = carry
        slot = tick - (segments - 1 - segment)
        active = (slot >= 0) & (slot < blocks)
        index = jnp.clip(slot, 0, blocks - 1)
        grad_out = jnp.where(segment == segments - 1, pick(seeds, index), incoming)
        x = pick(saved, index)
        down_t = pick(down_all, index)
        up_t = pick(up_all, index)

        def run():
            normed, low, inv = prepare(x, gain, down_t)
            return backward_core(x, normed, low, inv, grad_out, weight, gain, down_t, up_t)

        grad_in, seq_down, seq_up = lax.cond(
            active,
            run,
            lambda: (
                blank,
                jnp.zeros((rank, width), jnp.float32),
                jnp.zeros((rank, width), jnp.float32),
            ),
        )
        weights = pick(mix_all, index)[:, None, None]
        acc_down = acc_down + weights * seq_down[None]
        acc_up = acc_up + weights * seq_up[None]
        grads_in = place(grads_in, grad_in, index, active)
        return (grad_in, (grads_in, acc_down, acc_up))

    def backward_step(tick, carry):
        grad_in, rest = backward_tick(tick, carry)
        moved = shifted(grad_in, "segment", -1)
        return (moved,) + rest

    carry = (blank, stack_blank, acc_blank, acc_blank)
    carry = lax.fori_loop(0, ticks - 1, backward_step, carry)
    _, (grads_in, acc_down, acc_up) = backward_tick(ticks - 1, carry)
    grad_down, grad_up = side_by_side(
        (acc_down.astype(jnp.bfloat16), acc_up.astype(jnp.bfloat16)), "dp", 2, 0
    )
    return (outs[None, :, None], grads_in[None, :, None], grad_down[None], grad_up[None])


def solution(mesh):
    in_specs = (
        P(None, "dp", None, None),
        P("segment", "dp", None),
        P("segment", None),
        P("segment", None, None, None),
        P("segment", None, None, None),
        P(),
        P(),
        P(),
        P(None, "dp", None, None),
    )
    out_specs = (
        P("segment", None, "dp", None, None),
        P("segment", None, "dp", None, None),
        P("segment", None, None, "dp"),
        P("segment", None, None, "dp"),
    )
    return jax.shard_map(shards, mesh=mesh, in_specs=in_specs, out_specs=out_specs, check_vma=False)
```

profile of v0, /device:TPU:0, one launch (start us, length us, event | category | flops | bytes accessed | tf_op | source)
XLA Modules:
  0.0 870.6 jit_solution(13723919812734326416)
XLA Ops:
  13.2 3.1 bitcast_multiply_fusion
  16.4 193.5 %all-gather.3.cloned.1.call-done = bf16[1,4096,4096]{2,1,0:T(8,128)(2,1)} async-done(((bf16[1,256,4096]{2,1,0:T(8,128)(2,1)}), bf16[1,4096,4096]{2,1,0:T(8,128)(2,1)}) %all-gather.3.cloned.1.call-update) | async-done | bytes 33554448 | tf_op jit(solution)/shard_map/all_gather | solution.py:88
  212.8 230.3 %while.40 = (s32[]{:T(128)}, bf16[128,4096]{1,0:T(8,128)(2,1)}, bf16[2,128,4096]{2,1,0:T(8,128)(2,1)S(1)}, bf16[2,128,4096]{2,1,0:T(8,128)(2,1)}, s32[]{:T(128)}...) while((s32[]{:T(128)}, bf16[128,4096]{1,0:T(8,128)(2,1)}, ...), condition=%wide.region_5.6_spmd, body=%wide.region_1.5_spmd.sunk | while | flops 4321182720 | bytes 60985708 | solution.py:149
  214.7 23.2 %conditional.9 = (bf16[128,4096]{1,0:T(8,128)(2,1)}, bf16[1,128,4096]{2,1,0:T(8,128)(2,1)}) conditional(s32[]{:T(128)} %convert_element_type.345, () %tuple.153, (bf16[128,4096]{1,0:T(8,128)(2,1)S(1)}, f32[1,4096]{1,0:T(1,128)S(1)}, bf16[4096,4096]{1,0:T(8,128)(2,1)}, s32[]{:T(128)}, bf16[2,8,4096]{2,1,0:T(8,128)(2,1)S(1)}, ...), branch_computations={%region_2.2_spmd, %region_3.4_spmd} | conditional | flops 4319609856 | bytes 44207664 | solution.py:129
  215.0 16.5 %convolution_add_fusion.1 = f32[128,4096]{1,0:T(8,128)} fusion(bf16[4096,4096]{1,0:T(8,128)(2,1)} %get-tuple-element.684, bf16[128,4096]{1,0:T(8,128)(2,1)S(1)} %get-tuple-element.682, f32[4096]{0:T(1024)S(1)} %bitcast.186, f32[128]{0:T(128)S(1)} %add_rsqrt_fusion), kind=kOutput, calls=%fused_computation.1 | convolution fusion | flops 4298113024 | bytes 36717056 | tf_op jit(solution)/shard_map/while/body/eval_jaxpr/cond/branch_1_fun/dot_general | solution.py:45
  231.5 4.1 fusion
  239.2 2.8 select_dynamic-update-slice_fusion.4
  244.8 23.2 %conditional.9 = (bf16[128,4096]{1,0:T(8,128)(2,1)}, bf16[1,128,4096]{2,1,0:T(8,128)(2,1)}) conditional(s32[]{:T(128)} %convert_element_type.345, () %tuple.153, (bf16[128,4096]{1,0:T(8,128)(2,1)S(1)}, f32[1,4096]{1,0:T(1,128)S(1)}, bf16[4096,4096]{1,0:T(8,128)(2,1)}, s32[]{:T(128)}, bf16[2,8,4096]{2,1,0:T(8,128)(2,1)S(1)}, ...), branch_computations={%region_2.2_spmd, %region_3.4_spmd} | conditional | flops 4319609856 | bytes 44207664 | solution.py:129
  245.1 16.5 %convolution_add_fusion.1 = f32[128,4096]{1,0:T(8,128)} fusion(bf16[4096,4096]{1,0:T(8,128)(2,1)} %get-tuple-element.684, bf16[128,4096]{1,0:T(8,128)(2,1)S(1)} %get-tuple-element.682, f32[4096]{0:T(1024)S(1)} %bitcast.186, f32[128]{0:T(128)S(1)} %add_rsqrt_fusion), kind=kOutput, calls=%fused_computation.1 | convolution fusion | flops 4298113024 | bytes 36717056 | tf_op jit(solution)/shard_map/while/body/eval_jaxpr/cond/branch_1_fun/dot_general | solution.py:45
  261.6 4.1 fusion
  268.0 2.3 collective-permute-start
  270.2 2.8 select_dynamic-update-slice_fusion.4
  278.1 32.4 %collective-permute-start = (bf16[128,4096]{1,0:T(8,128)(2,1)}, bf16[128,4096]{1,0:T(8,128)(2,1)S(1)}, u32[]{:S(2)}, u32[]{:S(2)}) collective-permute-start(bf16[128,4096]{1,0:T(8,128)(2,1)} %get-tuple-element.1159), channel_id=1, source_target_pairs={{0,16},{16,32},{32,48},{48,64},{64,80},{80,96},{96,112},{1,17},{17... | collective-permute-start | bytes 3145736 | tf_op jit(solution)/shard_map/while/body/eval_jaxpr/ppermute | solution.py:12
  310.5 2.5 select_dynamic-update-slice_fusion.4
  318.0 14.1 %collective-permute-start = (bf16[128,4096]{1,0:T(8,128)(2,1)}, bf16[128,4096]{1,0:T(8,128)(2,1)S(1)}, u32[]{:S(2)}, u32[]{:S(2)}) collective-permute-start(bf16[128,4096]{1,0:T(8,128)(2,1)} %get-tuple-element.1159), channel_id=1, source_target_pairs={{0,16},{16,32},{32,48},{48,64},{64,80},{80,96},{96,112},{1,17},{17... | collective-permute-start | bytes 3145736 | tf_op jit(solution)/shard_map/while/body/eval_jaxpr/ppermute | solution.py:12
  332.1 2.5 select_dynamic-update-slice_fusion.4
  339.6 35.1 %collective-permute-start = (bf16[128,4096]{1,0:T(8,128)(2,1)}, bf16[128,4096]{1,0:T(8,128)(2,1)S(1)}, u32[]{:S(2)}, u32[]{:S(2)}) collective-permute-start(bf16[128,4096]{1,0:T(8,128)(2,1)} %get-tuple-element.1159), channel_id=1, source_target_pairs={{0,16},{16,32},{32,48},{48,64},{64,80},{80,96},{96,112},{1,17},{17... | collective-permute-start | bytes 3145736 | tf_op jit(solution)/shard_map/while/body/eval_jaxpr/ppermute | solution.py:12
  374.7 2.5 select_dynamic-update-slice_fusion.4
  382.3 14.1 %collective-permute-start = (bf16[128,4096]{1,0:T(8,128)(2,1)}, bf16[128,4096]{1,0:T(8,128)(2,1)S(1)}, u32[]{:S(2)}, u32[]{:S(2)}) collective-permute-start(bf16[128,4096]{1,0:T(8,128)(2,1)} %get-tuple-element.1159), channel_id=1, source_target_pairs={{0,16},{16,32},{32,48},{48,64},{64,80},{80,96},{96,112},{1,17},{17... | collective-permute-start | bytes 3145736 | tf_op jit(solution)/shard_map/while/body/eval_jaxpr/ppermute | solution.py:12
  396.4 2.5 select_dynamic-update-slice_fusion.4
  403.9 14.1 %collective-permute-start = (bf16[128,4096]{1,0:T(8,128)(2,1)}, bf16[128,4096]{1,0:T(8,128)(2,1)S(1)}, u32[]{:S(2)}, u32[]{:S(2)}) collective-permute-start(bf16[128,4096]{1,0:T(8,128)(2,1)} %get-tuple-element.1159), channel_id=1, source_target_pairs={{0,16},{16,32},{32,48},{48,64},{64,80},{80,96},{96,112},{1,17},{17... | collective-permute-start | bytes 3145736 | tf_op jit(solution)/shard_map/while/body/eval_jaxpr/ppermute | solution.py:12
  418.0 2.5 select_dynamic-update-slice_fusion.4
  425.5 14.1 %collective-permute-start = (bf16[128,4096]{1,0:T(8,128)(2,1)}, bf16[128,4096]{1,0:T(8,128)(2,1)S(1)}, u32[]{:S(2)}, u32[]{:S(2)}) collective-permute-start(bf16[128,4096]{1,0:T(8,128)(2,1)} %get-tuple-element.1159), channel_id=1, source_target_pairs={{0,16},{16,32},{32,48},{48,64},{64,80},{80,96},{96,112},{1,17},{17... | collective-permute-start | bytes 3145736 | tf_op jit(solution)/shard_map/while/body/eval_jaxpr/ppermute | solution.py:12
  439.6 2.5 select_dynamic-update-slice_fusion.4
  443.1 2.8 fusion.140
  448.6 355.2 %while.41 = (s32[]{:T(128)}, bf16[128,4096]{1,0:T(8,128)(2,1)}, bf16[2,128,4096]{2,1,0:T(8,128)(2,1)}, f32[16,8,4096]{2,1,0:T(8,128)}, f32[16,8,4096]{2,1,0:T(8,...) while((s32[]{:T(128)}, bf16[128,4096]{1,0:T(8,128)(2,1)}, ...), condition=%wide.region_14.15_spmd.clone, body=%wide.region_9.14_spmd.clone.sunk | while | flops 4354214400 | bytes 94118616 | solution.py:189
  448.6 2.3 conditional.10
  453.0 2.5 select_dynamic-update-slice_fusion.5
  455.5 2.7 select_add_fusion.3
  458.2 25.3 %collective-permute-done.1 = bf16[128,4096]{1,0:T(8,128)(2,1)S(1)} collective-permute-done((bf16[128,4096]{1,0:T(8,128)(2,1)}, bf16[128,4096]{1,0:T(8,128)(2,1)S(1)}, u32[]{:S(2)}, u32[]{:S(2)}) %collective-permute-start.1) | collective-permute-done | bytes 1048608 | tf_op jit(solution)/shard_map/while/body/eval_jaxpr/ppermute | solution.py:12
  484.4 2.3 conditional.10
  488.8 2.5 select_dynamic-update-slice_fusion.5
  491.3 4.3 select_add_fusion.3
  495.6 8.0 collective-permute-done.1
  504.6 2.3 conditional.10
  509.1 2.5 select_dynamic-update-slice_fusion.5
  511.6 4.3 select_add_fusion.3
  515.9 7.4 collective-permute-done.1
  524.2 2.3 conditional.10
  528.7 2.5 select_dynamic-update-slice_fusion.5
  531.2 4.3 select_add_fusion.3
  535.5 7.9 collective-permute-done.1
  544.3 2.3 conditional.10
  548.7 2.5 select_dynamic-update-slice_fusion.5
  551.2 4.3 select_add_fusion.3
  555.5 23.4 %collective-permute-done.1 = bf16[128,4096]{1,0:T(8,128)(2,1)S(1)} collective-permute-done((bf16[128,4096]{1,0:T(8,128)(2,1)}, bf16[128,4096]{1,0:T(8,128)(2,1)S(1)}, u32[]{:S(2)}, u32[]{:S(2)}) %collective-permute-start.1) | collective-permute-done | bytes 1048608 | tf_op jit(solution)/shard_map/while/body/eval_jaxpr/ppermute | solution.py:12
  584.3 2.5 select_dynamic-update-slice_fusion.5
  586.8 4.3 select_add_fusion.3
  591.1 8.0 collective-permute-done.1
  604.6 2.5 select_dynamic-update-slice_fusion.5
  607.0 4.3 select_add_fusion.3
  611.3 148.2 %collective-permute-done.1 = bf16[128,4096]{1,0:T(8,128)(2,1)S(1)} collective-permute-done((bf16[128,4096]{1,0:T(8,128)(2,1)}, bf16[128,4096]{1,0:T(8,128)(2,1)S(1)}, u32[]{:S(2)}, u32[]{:S(2)}) %collective-permute-start.1) | collective-permute-done | bytes 1048608 | tf_op jit(solution)/shard_map/while/body/eval_jaxpr/ppermute | solution.py:12
  760.5 25.9 %conditional.10 = (bf16[128,4096]{1,0:T(8,128)(2,1)}, f32[8,4096]{1,0:T(8,128)S(1)}, f32[8,4096]{1,0:T(8,128)S(1)}, bf16[1,128,4096]{2,1,0:T(8,128)(2,1)}) conditional(s32[]{:T(128)} %convert_element_type.346, () %tuple.157, (pred[]{:T(512)}, bf16[2,128,4096]{2,1,0:T(8,128)(2,1)}, s32[]{:T(128)}, bf16[128,4096]{1,0:T(8,128)(2,1)}, ...), branch_computations={%region_10.10_spmd, %region_11.13_spmd} | conditional | flops 4350544384 | bytes 57155172 | solution.py:168
  763.4 16.0 %fusion.153 = f32[128,4096]{1,0:T(8,128)S(1)} fusion(bf16[128,4096]{1,0:T(8,128)(2,1)S(1)} %bitcast_select_fusion.2, bf16[4096,4096]{1,0:T(8,128)(2,1)} %get-tuple-element.714), kind=kOutput, calls=%fused_computation.169 | convolution fusion | flops 4294967296 | bytes 36700160 | tf_op jit(solution)/shard_map/while/body/eval_jaxpr/cond/branch_1_fun/dot_general | solution.py:52
  782.1 2.3 copy.64
  788.6 2.8 select_dynamic-update-slice_fusion.5
  791.4 4.3 select_add_fusion.3
  795.7 7.1 collective-permute-done.1
  803.8 23.6 %conditional.5 = (f32[8,4096]{1,0:T(8,128)}, f32[8,4096]{1,0:T(8,128)}, bf16[1,128,4096]{2,1,0:T(8,128)(2,1)}) conditional(s32[]{:T(128)} %convert_element_type.171, () %tuple.98, (pred[]{:T(512)}, bf16[2,128,4096]{2,1,0:T(8,128)(2,1)}, s32[]{:T(128)}, bf16[128,4096]{1,0:T(8,128)(2,1)}, bf16[2,8,4096]{2,0,1:T(2,128)(2,1)}, ...), branch_computations={%region_15.16_spmd, %region_16.19_spmd} | conditional | flops 4350544384 | bytes 56620128 | solution.py:168
  805.9 16.0 %fusion.154 = f32[128,4096]{1,0:T(8,128)S(1)} fusion(bf16[128,4096]{1,0:T(8,128)(2,1)S(1)} %bitcast_select_fusion.3, bf16[4096,4096]{1,0:T(8,128)(2,1)} %get-tuple-element.744), kind=kOutput, calls=%fused_computation.170 | convolution fusion | flops 4294967296 | bytes 36700160 | tf_op jit(solution)/shard_map/cond/branch_1_fun/dot_general | solution.py:52
  827.3 2.8 add_convert_fusion.1
  833.1 5.5 all-to-all-start
  843.7 4.0 bitcast_dynamic-update-slice_fusion
  847.8 13.3 %all-to-all-done = bf16[16,32,8,256]{3,2,1,0:T(8,128)(2,1)} async-done(((bf16[16,32,8,256]{3,2,1,0:T(8,128)(2,1)}), bf16[16,32,8,256]{3,2,1,0:T(8,128)(2,1)}, u32[]{:S(2)}, u32[]{:S(2)}) %all-to-all-start) | async-done | bytes 2097184 | tf_op jit(solution)/shard_map/all_to_all | solution.py:22
  (234 shorter events, 138.4 us)
Async XLA Ops:
  7.2 1.3 copy-start
  7.2 1.0 copy-start.18
  7.2 2.9 copy-start.16
  7.2 202.7 %all-gather.3.cloned.1.call-start = ((), (), s32[]{:S(2)}) async-start(), calls=%async_computation.1 | async-start | bytes 35651584 | tf_op jit(solution)/shard_map/all_gather | solution.py:88
  7.9 4.5 copy-start.23
  8.5 7.9 copy-start.21
  10.1 6.3 copy-start.10
  11.7 4.6 copy-start.13
  210.1 2.7 copy-start.9
  237.8 4.1 collective-permute-start
  242.0 1.0 copy-start.7
  268.0 5.1 collective-permute-start
  273.1 1.0 copy-start.7
  278.1 34.9 %collective-permute-start = (bf16[128,4096]{1,0:T(8,128)(2,1)}, bf16[128,4096]{1,0:T(8,128)(2,1)S(1)}, u32[]{:S(2)}, u32[]{:S(2)}) collective-permute-start(bf16[128,4096]{1,0:T(8,128)(2,1)} %get-tuple-element.1159), channel_id=1, source_target_pairs={{0,16},{16,32},{32,48},{48,64},{64,80},{80,96},{96,112},{1,17},{17... | collective-permute-start | bytes 3145736 | tf_op jit(solution)/shard_map/while/body/eval_jaxpr/ppermute | solution.py:12
  313.0 1.0 copy-start.7
  318.0 16.6 %collective-permute-start = (bf16[128,4096]{1,0:T(8,128)(2,1)}, bf16[128,4096]{1,0:T(8,128)(2,1)S(1)}, u32[]{:S(2)}, u32[]{:S(2)}) collective-permute-start(bf16[128,4096]{1,0:T(8,128)(2,1)} %get-tuple-element.1159), channel_id=1, source_target_pairs={{0,16},{16,32},{32,48},{48,64},{64,80},{80,96},{96,112},{1,17},{17... | collective-permute-start | bytes 3145736 | tf_op jit(solution)/shard_map/while/body/eval_jaxpr/ppermute | solution.py:12
  334.6 1.0 copy-start.7
  339.6 37.6 %collective-permute-start = (bf16[128,4096]{1,0:T(8,128)(2,1)}, bf16[128,4096]{1,0:T(8,128)(2,1)S(1)}, u32[]{:S(2)}, u32[]{:S(2)}) collective-permute-start(bf16[128,4096]{1,0:T(8,128)(2,1)} %get-tuple-element.1159), channel_id=1, source_target_pairs={{0,16},{16,32},{32,48},{48,64},{64,80},{80,96},{96,112},{1,17},{17... | collective-permute-start | bytes 3145736 | tf_op jit(solution)/shard_map/while/body/eval_jaxpr/ppermute | solution.py:12
  377.3 1.0 copy-start.7
  382.3 16.6 %collective-permute-start = (bf16[128,4096]{1,0:T(8,128)(2,1)}, bf16[128,4096]{1,0:T(8,128)(2,1)S(1)}, u32[]{:S(2)}, u32[]{:S(2)}) collective-permute-start(bf16[128,4096]{1,0:T(8,128)(2,1)} %get-tuple-element.1159), channel_id=1, source_target_pairs={{0,16},{16,32},{32,48},{48,64},{64,80},{80,96},{96,112},{1,17},{17... | collective-permute-start | bytes 3145736 | tf_op jit(solution)/shard_map/while/body/eval_jaxpr/ppermute | solution.py:12
  398.9 1.0 copy-start.7
  403.9 16.6 %collective-permute-start = (bf16[128,4096]{1,0:T(8,128)(2,1)}, bf16[128,4096]{1,0:T(8,128)(2,1)S(1)}, u32[]{:S(2)}, u32[]{:S(2)}) collective-permute-start(bf16[128,4096]{1,0:T(8,128)(2,1)} %get-tuple-element.1159), channel_id=1, source_target_pairs={{0,16},{16,32},{32,48},{48,64},{64,80},{80,96},{96,112},{1,17},{17... | collective-permute-start | bytes 3145736 | tf_op jit(solution)/shard_map/while/body/eval_jaxpr/ppermute | solution.py:12
  420.5 1.0 copy-start.7
  425.5 16.6 %collective-permute-start = (bf16[128,4096]{1,0:T(8,128)(2,1)}, bf16[128,4096]{1,0:T(8,128)(2,1)S(1)}, u32[]{:S(2)}, u32[]{:S(2)}) collective-permute-start(bf16[128,4096]{1,0:T(8,128)(2,1)} %get-tuple-element.1159), channel_id=1, source_target_pairs={{0,16},{16,32},{32,48},{48,64},{64,80},{80,96},{96,112},{1,17},{17... | collective-permute-start | bytes 3145736 | tf_op jit(solution)/shard_map/while/body/eval_jaxpr/ppermute | solution.py:12
  442.1 1.0 copy-start.7
  450.8 32.6 %collective-permute-start.1 = (bf16[128,4096]{1,0:T(8,128)(2,1)}, bf16[128,4096]{1,0:T(8,128)(2,1)S(1)}, u32[]{:S(2)}, u32[]{:S(2)}) collective-permute-start(bf16[128,4096]{1,0:T(8,128)(2,1)} %get-tuple-element.1176), channel_id=1, source_target_pairs={{16,0},{32,16},{48,32},{64,48},{80,64},{96,80},{112,96},{17,1},{33... | collective-permute-start | bytes 3145736 | tf_op jit(solution)/shard_map/while/body/eval_jaxpr/ppermute | solution.py:12
  452.1 3.3 copy-start.2
  458.2 25.3 %copy-start.3 = (f32[16,8,4096]{2,1,0:T(8,128)}, f32[16,8,4096]{2,1,0:T(8,128)S(1)}, u32[]{:S(2)}) copy-start(f32[16,8,4096]{2,1,0:T(8,128)S(1)} %get-tuple-element.1273) | copy-start | bytes 6291460 | tf_op jit(solution)/shard_map/while
  483.4 1.0 copy-start.6
  486.7 17.0 %collective-permute-start.1 = (bf16[128,4096]{1,0:T(8,128)(2,1)}, bf16[128,4096]{1,0:T(8,128)(2,1)S(1)}, u32[]{:S(2)}, u32[]{:S(2)}) collective-permute-start(bf16[128,4096]{1,0:T(8,128)(2,1)} %get-tuple-element.1176), channel_id=1, source_target_pairs={{16,0},{32,16},{48,32},{64,48},{80,64},{96,80},{112,96},{17,1},{33... | collective-permute-start | bytes 3145736 | tf_op jit(solution)/shard_map/while/body/eval_jaxpr/ppermute | solution.py:12
  488.0 3.3 copy-start.2
  495.6 8.1 copy-start.3
  503.7 1.0 copy-start.6
  506.9 16.3 %collective-permute-start.1 = (bf16[128,4096]{1,0:T(8,128)(2,1)}, bf16[128,4096]{1,0:T(8,128)(2,1)S(1)}, u32[]{:S(2)}, u32[]{:S(2)}) collective-permute-start(bf16[128,4096]{1,0:T(8,128)(2,1)} %get-tuple-element.1176), channel_id=1, source_target_pairs={{16,0},{32,16},{48,32},{64,48},{80,64},{96,80},{112,96},{17,1},{33... | collective-permute-start | bytes 3145736 | tf_op jit(solution)/shard_map/while/body/eval_jaxpr/ppermute | solution.py:12
  508.2 3.3 copy-start.2
  515.9 7.4 copy-start.3
  526.5 16.8 %collective-permute-start.1 = (bf16[128,4096]{1,0:T(8,128)(2,1)}, bf16[128,4096]{1,0:T(8,128)(2,1)S(1)}, u32[]{:S(2)}, u32[]{:S(2)}) collective-permute-start(bf16[128,4096]{1,0:T(8,128)(2,1)} %get-tuple-element.1176), channel_id=1, source_target_pairs={{16,0},{32,16},{48,32},{64,48},{80,64},{96,80},{112,96},{17,1},{33... | collective-permute-start | bytes 3145736 | tf_op jit(solution)/shard_map/while/body/eval_jaxpr/ppermute | solution.py:12
  527.8 3.3 copy-start.2
  535.4 7.9 copy-start.3
  546.6 32.3 %collective-permute-start.1 = (bf16[128,4096]{1,0:T(8,128)(2,1)}, bf16[128,4096]{1,0:T(8,128)(2,1)S(1)}, u32[]{:S(2)}, u32[]{:S(2)}) collective-permute-start(bf16[128,4096]{1,0:T(8,128)(2,1)} %get-tuple-element.1176), channel_id=1, source_target_pairs={{16,0},{32,16},{48,32},{64,48},{80,64},{96,80},{112,96},{17,1},{33... | collective-permute-start | bytes 3145736 | tf_op jit(solution)/shard_map/while/body/eval_jaxpr/ppermute | solution.py:12
  547.9 3.3 copy-start.2
  555.5 23.4 %copy-start.3 = (f32[16,8,4096]{2,1,0:T(8,128)}, f32[16,8,4096]{2,1,0:T(8,128)S(1)}, u32[]{:S(2)}) copy-start(f32[16,8,4096]{2,1,0:T(8,128)S(1)} %get-tuple-element.1273) | copy-start | bytes 6291460 | tf_op jit(solution)/shard_map/while
  578.9 1.0 copy-start.6
  582.2 17.0 %collective-permute-start.1 = (bf16[128,4096]{1,0:T(8,128)(2,1)}, bf16[128,4096]{1,0:T(8,128)(2,1)S(1)}, u32[]{:S(2)}, u32[]{:S(2)}) collective-permute-start(bf16[128,4096]{1,0:T(8,128)(2,1)} %get-tuple-element.1176), channel_id=1, source_target_pairs={{16,0},{32,16},{48,32},{64,48},{80,64},{96,80},{112,96},{17,1},{33... | collective-permute-start | bytes 3145736 | tf_op jit(solution)/shard_map/while/body/eval_jaxpr/ppermute | solution.py:12
  583.5 3.3 copy-start.2
  591.1 8.1 copy-start.3
  602.4 157.1 %collective-permute-start.1 = (bf16[128,4096]{1,0:T(8,128)(2,1)}, bf16[128,4096]{1,0:T(8,128)(2,1)S(1)}, u32[]{:S(2)}, u32[]{:S(2)}) collective-permute-start(bf16[128,4096]{1,0:T(8,128)(2,1)} %get-tuple-element.1176), channel_id=1, source_target_pairs={{16,0},{32,16},{48,32},{64,48},{80,64},{96,80},{112,96},{17,1},{33... | collective-permute-start | bytes 3145736 | tf_op jit(solution)/shard_map/while/body/eval_jaxpr/ppermute | solution.py:12
  603.7 3.3 copy-start.2
  611.3 148.2 %copy-start.3 = (f32[16,8,4096]{2,1,0:T(8,128)}, f32[16,8,4096]{2,1,0:T(8,128)S(1)}, u32[]{:S(2)}) copy-start(f32[16,8,4096]{2,1,0:T(8,128)S(1)} %get-tuple-element.1273) | copy-start | bytes 6291460 | tf_op jit(solution)/shard_map/while
  759.6 1.0 copy-start.6
  763.4 16.0 %copy-start.17 = (bf16[128,8]{0,1:T(8,128)(2,1)}, bf16[128,8]{0,1:T(8,128)(2,1)S(1)}, u32[]{:S(2)}) copy-start(bf16[128,8]{0,1:T(8,128)(2,1)S(1)} %convolution_convert_fusion.1) | copy-start | bytes 6148 | tf_op jit(solution)/shard_map/while/body/eval_jaxpr/cond
  780.2 4.2 copy-start.19
  786.5 16.3 %collective-permute-start.1 = (bf16[128,4096]{1,0:T(8,128)(2,1)}, bf16[128,4096]{1,0:T(8,128)(2,1)S(1)}, u32[]{:S(2)}, u32[]{:S(2)}) collective-permute-start(bf16[128,4096]{1,0:T(8,128)(2,1)} %get-tuple-element.1176), channel_id=1, source_target_pairs={{16,0},{32,16},{48,32},{64,48},{80,64},{96,80},{112,96},{17,1},{33... | collective-permute-start | bytes 3145736 | tf_op jit(solution)/shard_map/while/body/eval_jaxpr/ppermute | solution.py:12
  787.7 3.6 copy-start.2
  795.7 7.1 copy-start.3
  803.8 1.7 copy-start.15
  805.9 16.0 %copy-start.12 = (bf16[2,8,4096]{2,0,1:T(2,128)(2,1)S(1)}, bf16[2,8,4096]{2,0,1:T(2,128)(2,1)}, u32[]{:S(2)}) copy-start(bf16[2,8,4096]{2,0,1:T(2,128)(2,1)} %get-tuple-element.936) | copy-start | bytes 393220 | tf_op jit(solution)/shard_map/cond
  833.1 5.5 copy-start.4
  833.1 28.0 %all-to-all-start = ((bf16[16,32,8,256]{3,2,1,0:T(8,128)(2,1)}), bf16[16,32,8,256]{3,2,1,0:T(8,128)(2,1)}, u32[]{:S(2)}, u32[]{:S(2)}) async-start(bf16[16,32,8,256]{3,2,1,0:T(8,128)(2,1)} %copy.43), calls=%async_computation | async-start | bytes 4194304 | tf_op jit(solution)/shard_map/all_to_all | solution.py:22
  838.7 2.3 copy-start.5
  838.7 2.6 copy-start.8
  838.7 2.6 copy-start.11
  838.7 2.6 copy-start.14
  843.7 20.0 %copy-start.1 = (bf16[1,16,8,4096]{3,2,1,0:T(8,128)(2,1)S(1)}, bf16[1,16,8,4096]{3,2,1,0:T(8,128)(2,1)}, u32[]{:S(2)}) copy-start(bf16[1,16,8,4096]{3,2,1,0:T(8,128)(2,1)} %param.24) | copy-start | bytes 3145732
  (5 other events, 4.7 us)
Sparse Core Ops, SparseCore 0:
  10.2 199.6 all-gather.2
where the time goes:
time: 873 us; the launch traced here: 871 us
  waiting for transfers between devices  443 us (51%)
  starting transfers between devices  143 us (16%)
  other arithmetic  111 us (13%)
  matrix products  84.4 us (10%)
  local copies, waits for them, and re-layouts  74.1 us (8%)
  between operations  14.3 us (2%)
    ppermute x16, waiting for transfers between devices, shifted(): return lax.ppermute(block, axis, route)  235 us
    all_gather x1, waiting for transfers between devices, shards(): weight = lax.all_gather(base_weight[0], 'dp', axis=0, tiled=True)  194 us
    ppermute x16, starting transfers between devices, shifted(): return lax.ppermute(block, axis, route)  138 us
    select_n x26, other arithmetic, place(): jnp.where(active, lax.dynamic_update_index_in_dim(table, value, index, 0)...  62.3 us
    dot_general x2, matrix products, forward_full(): jnp.dot(normed, weight, preferred_element_type=jnp.float32)  33 us
    add x8, other arithmetic, backward_tick(): acc_up = acc_up + weights * seq_up[None]  32.8 us
    dot_general x2, matrix products, backward_core(): dnorm = jnp.dot(grad_out, weight.T, preferred_element_type=jnp.float32)  32 us
  transfers between devices with their start and end apart: 18, of which 10 were waited for; matrix products, arithmetic and copies ran while one was open for 11% of the time, Pallas kernels for 0%

commit v1 on v0

--- a/solution.py
+++ b/solution.py
@@ -85,7 +85,15 @@
     segments = lax.axis_size("segment")
     segment = lax.axis_index("segment")
     member = lax.axis_index("dp")
-    weight = lax.all_gather(base_weight[0], "dp", axis=0, tiled=True)
+    weight = jnp.concatenate(
+        lax.all_to_all(
+            jnp.stack([base_weight[0]] * lax.axis_size("dp")),
+            axis_name="dp",
+            split_axis=0,
+            concat_axis=0,
+        ),
+        0,
+    )
     gain = norm_gain[0]
     micro = embeds.shape[0]
     rows = embeds.shape[2]

time: 873 us -> 1180 us (1.35)
  waiting for transfers between devices: 443 us -> 742 us
  between operations: 14.3 us -> 0.92 us
  local copies, waits for them, and re-layouts: 74.1 us -> 86.5 us
    all_to_all x0 -> x1, waiting for transfers between devices: none -> 493 us  [shards(): lax.all_to_all(jnp.stack([base_weight[0]] * lax.axis_size('dp')), axis_na...]
    all_gather x1 -> x0, waiting for transfers between devices: 194 us -> none  [shards(): weight = lax.all_gather(base_weight[0], 'dp', axis=0, tiled=True)]
    another operation x16 -> x17, local copies, waits for them, and re-layouts: 0.3 us -> 12.5 us  [the longest x1 12.2 us: shards(): jnp.stack([base_weight[0]] * lax.axis_size('dp'))]
  transfers between devices with their start and end apart: 18 -> 18, of which waited for: 10 -> 10; matrix products, arithmetic and copies ran while one was open for 11% -> 8% of each run, Pallas kernels for 0% -> 0%
where the time goes in v1:
time: 1180 us
  waiting for transfers between devices  742 us (63%)
  starting transfers between devices  151 us (13%)
  other arithmetic  111 us (9%)
  local copies, waits for them, and re-layouts  86.5 us (7%)
  matrix products  84.2 us (7%)
    all_to_all x1, waiting for transfers between devices, shards(): lax.all_to_all(jnp.stack([base_weight[0]] * lax.axis_size('dp')), axis_na...  493 us
    ppermute x16, waiting for transfers between devices, shifted(): return lax.ppermute(block, axis, route)  235 us
    ppermute x16, starting transfers between devices, shifted(): return lax.ppermute(block, axis, route)  138 us
    select_n x26, other arithmetic, place(): jnp.where(active, lax.dynamic_update_index_in_dim(table, value, index, 0)...  62.2 us
    dot_general x2, matrix products, forward_full(): jnp.dot(normed, weight, preferred_element_type=jnp.float32)  32.9 us
    add x8, other arithmetic, backward_tick(): acc_up = acc_up + weights * seq_up[None]  32.8 us
    dot_general x2, matrix products, backward_core(): dnorm = jnp.dot(grad_out, weight.T, preferred_element_type=jnp.float32)  32 us
  transfers between devices with their start and end apart: 18, of which 10 were waited for; matrix products, arithmetic and copies ran while one was open for 8% of the time, Pallas kernels for 0%

profile of v1, /device:TPU:0, one launch (start us, length us, event | category | flops | bytes accessed | tf_op | source)
XLA Modules:
  0.0 1175.2 jit_solution(14291795063509352815)
XLA Ops:
  0.6 12.2 %stack.3 = bf16[16,256,4096]{2,1,0:T(8,128)(2,1)} broadcast(bf16[256,4096]{1,0:T(8,128)(2,1)} %bitcast.198), dimensions={1,2} | broadcast | bytes 35651584 | tf_op jit(solution)/shard_map/stack | solution.py:90
  12.9 8.3 all-to-all-start
  26.6 3.1 bitcast_multiply_fusion
  29.7 493.2 %all-to-all-done = bf16[16,256,4096]{2,1,0:T(8,128)(2,1)} async-done(((bf16[16,256,4096]{2,1,0:T(8,128)(2,1)}), bf16[16,256,4096]{2,1,0:T(8,128)(2,1)}, u32[]{:S(2)}, u32[]{:S(2)}) %all-to-all-start) | async-done | bytes 33554464 | tf_op jit(solution)/shard_map/all_to_all | solution.py:89
  525.9 230.5 %while.40 = (s32[]{:T(128)}, bf16[128,4096]{1,0:T(8,128)(2,1)}, bf16[2,128,4096]{2,1,0:T(8,128)(2,1)S(1)}, bf16[2,128,4096]{2,1,0:T(8,128)(2,1)}, s32[]{:T(128)}...) while((s32[]{:T(128)}, bf16[128,4096]{1,0:T(8,128)(2,1)}, ...), condition=%wide.region_5.6_spmd, body=%wide.region_1.5_spmd.sunk | while | flops 4321182720 | bytes 60985708 | solution.py:157
  527.7 23.1 %conditional.9 = (bf16[128,4096]{1,0:T(8,128)(2,1)}, bf16[1,128,4096]{2,1,0:T(8,128)(2,1)}) conditional(s32[]{:T(128)} %convert_element_type.345, () %tuple.153, (bf16[128,4096]{1,0:T(8,128)(2,1)S(1)}, f32[1,4096]{1,0:T(1,128)S(1)}, bf16[4096,4096]{1,0:T(8,128)(2,1)}, s32[]{:T(128)}, bf16[2,8,4096]{2,1,0:T(8,128)(2,1)S(1)}, ...), branch_computations={%region_2.2_spmd, %region_3.4_spmd} | conditional | flops 4319609856 | bytes 44207664 | solution.py:137
  528.0 16.4 %convolution_add_fusion.1 = f32[128,4096]{1,0:T(8,128)} fusion(bf16[4096,4096]{1,0:T(8,128)(2,1)} %get-tuple-element.684, bf16[128,4096]{1,0:T(8,128)(2,1)S(1)} %get-tuple-element.682, f32[4096]{0:T(1024)S(1)} %bitcast.186, f32[128]{0:T(128)S(1)} %add_rsqrt_fusion), kind=kOutput, calls=%fused_computation.1 | convolution fusion | flops 4298113024 | bytes 36717056 | tf_op jit(solution)/shard_map/while/body/eval_jaxpr/cond/branch_1_fun/dot_general | solution.py:45
  544.5 4.1 fusion
  548.5 2.3 copy.55
  552.2 2.8 select_dynamic-update-slice_fusion.4
  557.8 23.1 %conditional.9 = (bf16[128,4096]{1,0:T(8,128)(2,1)}, bf16[1,128,4096]{2,1,0:T(8,128)(2,1)}) conditional(s32[]{:T(128)} %convert_element_type.345, () %tuple.153, (bf16[128,4096]{1,0:T(8,128)(2,1)S(1)}, f32[1,4096]{1,0:T(1,128)S(1)}, bf16[4096,4096]{1,0:T(8,128)(2,1)}, s32[]{:T(128)}, bf16[2,8,4096]{2,1,0:T(8,128)(2,1)S(1)}, ...), branch_computations={%region_2.2_spmd, %region_3.4_spmd} | conditional | flops 4319609856 | bytes 44207664 | solution.py:137
  558.1 16.4 %convolution_add_fusion.1 = f32[128,4096]{1,0:T(8,128)} fusion(bf16[4096,4096]{1,0:T(8,128)(2,1)} %get-tuple-element.684, bf16[128,4096]{1,0:T(8,128)(2,1)S(1)} %get-tuple-element.682, f32[4096]{0:T(1024)S(1)} %bitcast.186, f32[128]{0:T(128)S(1)} %add_rsqrt_fusion), kind=kOutput, calls=%fused_computation.1 | convolution fusion | flops 4298113024 | bytes 36717056 | tf_op jit(solution)/shard_map/while/body/eval_jaxpr/cond/branch_1_fun/dot_general | solution.py:45
  574.6 4.1 fusion
  578.6 2.3 copy.55
  581.0 2.3 collective-permute-start
  583.2 2.8 select_dynamic-update-slice_fusion.4
  588.9 2.2 conditional.9
  591.1 32.3 %collective-permute-start = (bf16[128,4096]{1,0:T(8,128)(2,1)}, bf16[128,4096]{1,0:T(8,128)(2,1)S(1)}, u32[]{:S(2)}, u32[]{:S(2)}) collective-permute-start(bf16[128,4096]{1,0:T(8,128)(2,1)} %get-tuple-element.1159), channel_id=1, source_target_pairs={{0,16},{16,32},{32,48},{48,64},{64,80},{80,96},{96,112},{1,17},{17... | collective-permute-start | bytes 3145736 | tf_op jit(solution)/shard_map/while/body/eval_jaxpr/ppermute | solution.py:12
  623.5 2.5 select_dynamic-update-slice_fusion.4
  631.1 14.1 %collective-permute-start = (bf16[128,4096]{1,0:T(8,128)(2,1)}, bf16[128,4096]{1,0:T(8,128)(2,1)S(1)}, u32[]{:S(2)}, u32[]{:S(2)}) collective-permute-start(bf16[128,4096]{1,0:T(8,128)(2,1)} %get-tuple-element.1159), channel_id=1, source_target_pairs={{0,16},{16,32},{32,48},{48,64},{64,80},{80,96},{96,112},{1,17},{17... | collective-permute-start | bytes 3145736 | tf_op jit(solution)/shard_map/while/body/eval_jaxpr/ppermute | solution.py:12
  645.2 2.5 select_dynamic-update-slice_fusion.4
  652.7 35.0 %collective-permute-start = (bf16[128,4096]{1,0:T(8,128)(2,1)}, bf16[128,4096]{1,0:T(8,128)(2,1)S(1)}, u32[]{:S(2)}, u32[]{:S(2)}) collective-permute-start(bf16[128,4096]{1,0:T(8,128)(2,1)} %get-tuple-element.1159), channel_id=1, source_target_pairs={{0,16},{16,32},{32,48},{48,64},{64,80},{80,96},{96,112},{1,17},{17... | collective-permute-start | bytes 3145736 | tf_op jit(solution)/shard_map/while/body/eval_jaxpr/ppermute | solution.py:12
  687.8 2.5 select_dynamic-update-slice_fusion.4
  695.3 14.1 %collective-permute-start = (bf16[128,4096]{1,0:T(8,128)(2,1)}, bf16[128,4096]{1,0:T(8,128)(2,1)S(1)}, u32[]{:S(2)}, u32[]{:S(2)}) collective-permute-start(bf16[128,4096]{1,0:T(8,128)(2,1)} %get-tuple-element.1159), channel_id=1, source_target_pairs={{0,16},{16,32},{32,48},{48,64},{64,80},{80,96},{96,112},{1,17},{17... | collective-permute-start | bytes 3145736 | tf_op jit(solution)/shard_map/while/body/eval_jaxpr/ppermute | solution.py:12
  709.5 2.5 select_dynamic-update-slice_fusion.4
  717.0 14.1 %collective-permute-start = (bf16[128,4096]{1,0:T(8,128)(2,1)}, bf16[128,4096]{1,0:T(8,128)(2,1)S(1)}, u32[]{:S(2)}, u32[]{:S(2)}) collective-permute-start(bf16[128,4096]{1,0:T(8,128)(2,1)} %get-tuple-element.1159), channel_id=1, source_target_pairs={{0,16},{16,32},{32,48},{48,64},{64,80},{80,96},{96,112},{1,17},{17... | collective-permute-start | bytes 3145736 | tf_op jit(solution)/shard_map/while/body/eval_jaxpr/ppermute | solution.py:12
  731.1 2.5 select_dynamic-update-slice_fusion.4
  738.7 14.1 %collective-permute-start = (bf16[128,4096]{1,0:T(8,128)(2,1)}, bf16[128,4096]{1,0:T(8,128)(2,1)S(1)}, u32[]{:S(2)}, u32[]{:S(2)}) collective-permute-start(bf16[128,4096]{1,0:T(8,128)(2,1)} %get-tuple-element.1159), channel_id=1, source_target_pairs={{0,16},{16,32},{32,48},{48,64},{64,80},{80,96},{96,112},{1,17},{17... | collective-permute-start | bytes 3145736 | tf_op jit(solution)/shard_map/while/body/eval_jaxpr/ppermute | solution.py:12
  752.8 2.5 select_dynamic-update-slice_fusion.4
  756.4 2.8 fusion.140
  761.8 354.4 %while.41 = (s32[]{:T(128)}, bf16[128,4096]{1,0:T(8,128)(2,1)}, bf16[2,128,4096]{2,1,0:T(8,128)(2,1)}, f32[16,8,4096]{2,1,0:T(8,128)}, f32[16,8,4096]{2,1,0:T(8,...) while((s32[]{:T(128)}, bf16[128,4096]{1,0:T(8,128)(2,1)}, ...), condition=%wide.region_14.15_spmd.clone, body=%wide.region_9.14_spmd.clone.sunk | while | flops 4354214400 | bytes 94118616 | solution.py:197
  766.2 2.5 select_dynamic-update-slice_fusion.5
  768.7 2.7 select_add_fusion.3
  771.4 25.1 %collective-permute-done.1 = bf16[128,4096]{1,0:T(8,128)(2,1)S(1)} collective-permute-done((bf16[128,4096]{1,0:T(8,128)(2,1)}, bf16[128,4096]{1,0:T(8,128)(2,1)S(1)}, u32[]{:S(2)}, u32[]{:S(2)}) %collective-permute-start.1) | collective-permute-done | bytes 1048608 | tf_op jit(solution)/shard_map/while/body/eval_jaxpr/ppermute | solution.py:12
  801.8 2.5 select_dynamic-update-slice_fusion.5
  804.3 4.3 select_add_fusion.3
  808.6 8.1 collective-permute-done.1
  822.0 2.5 select_dynamic-update-slice_fusion.5
  824.5 4.3 select_add_fusion.3
  828.8 7.4 collective-permute-done.1
  841.6 2.5 select_dynamic-update-slice_fusion.5
  844.0 4.3 select_add_fusion.3
  848.3 7.9 collective-permute-done.1
  861.6 2.5 select_dynamic-update-slice_fusion.5
  864.0 4.3 select_add_fusion.3
  868.3 23.3 %collective-permute-done.1 = bf16[128,4096]{1,0:T(8,128)(2,1)S(1)} collective-permute-done((bf16[128,4096]{1,0:T(8,128)(2,1)}, bf16[128,4096]{1,0:T(8,128)(2,1)S(1)}, u32[]{:S(2)}, u32[]{:S(2)}) %collective-permute-start.1) | collective-permute-done | bytes 1048608 | tf_op jit(solution)/shard_map/while/body/eval_jaxpr/ppermute | solution.py:12
  897.0 2.5 select_dynamic-update-slice_fusion.5
  899.5 4.3 select_add_fusion.3
  903.8 8.1 collective-permute-done.1
  917.2 2.5 select_dynamic-update-slice_fusion.5
  919.6 4.3 select_add_fusion.3
  923.9 148.1 %collective-permute-done.1 = bf16[128,4096]{1,0:T(8,128)(2,1)S(1)} collective-permute-done((bf16[128,4096]{1,0:T(8,128)(2,1)}, bf16[128,4096]{1,0:T(8,128)(2,1)S(1)}, u32[]{:S(2)}, u32[]{:S(2)}) %collective-permute-start.1) | collective-permute-done | bytes 1048608 | tf_op jit(solution)/shard_map/while/body/eval_jaxpr/ppermute | solution.py:12
  1073.1 25.8 %conditional.10 = (bf16[128,4096]{1,0:T(8,128)(2,1)}, f32[8,4096]{1,0:T(8,128)S(1)}, f32[8,4096]{1,0:T(8,128)S(1)}, bf16[1,128,4096]{2,1,0:T(8,128)(2,1)}) conditional(s32[]{:T(128)} %convert_element_type.346, () %tuple.157, (pred[]{:T(512)}, bf16[2,128,4096]{2,1,0:T(8,128)(2,1)}, s32[]{:T(128)}, bf16[128,4096]{1,0:T(8,128)(2,1)}, ...), branch_computations={%region_10.10_spmd, %region_11.13_spmd} | conditional | flops 4350544384 | bytes 57155172 | solution.py:176
  1076.0 16.0 %fusion.153 = f32[128,4096]{1,0:T(8,128)S(1)} fusion(bf16[128,4096]{1,0:T(8,128)(2,1)S(1)} %bitcast_select_fusion.2, bf16[4096,4096]{1,0:T(8,128)(2,1)} %get-tuple-element.714), kind=kOutput, calls=%fused_computation.169 | convolution fusion | flops 4294967296 | bytes 36700160 | tf_op jit(solution)/shard_map/while/body/eval_jaxpr/cond/branch_1_fun/dot_general | solution.py:52
  1094.6 2.3 copy.64
  1101.1 2.8 select_dynamic-update-slice_fusion.5
  1103.8 4.3 select_add_fusion.3
  1108.1 7.1 collective-permute-done.1
  1116.2 23.6 %conditional.5 = (f32[8,4096]{1,0:T(8,128)}, f32[8,4096]{1,0:T(8,128)}, bf16[1,128,4096]{2,1,0:T(8,128)(2,1)}) conditional(s32[]{:T(128)} %convert_element_type.171, () %tuple.98, (pred[]{:T(512)}, bf16[2,128,4096]{2,1,0:T(8,128)(2,1)}, s32[]{:T(128)}, bf16[128,4096]{1,0:T(8,128)(2,1)}, bf16[2,8,4096]{2,0,1:T(2,128)(2,1)}, ...), branch_computations={%region_15.16_spmd, %region_16.19_spmd} | conditional | flops 4350544384 | bytes 56620128 | solution.py:176
  1118.4 16.0 %fusion.154 = f32[128,4096]{1,0:T(8,128)S(1)} fusion(bf16[128,4096]{1,0:T(8,128)(2,1)S(1)} %bitcast_select_fusion.3, bf16[4096,4096]{1,0:T(8,128)(2,1)} %get-tuple-element.744), kind=kOutput, calls=%fused_computation.170 | convolution fusion | flops 4294967296 | bytes 36700160 | tf_op jit(solution)/shard_map/cond/branch_1_fun/dot_general | solution.py:52
  1139.8 2.8 add_convert_fusion.1
  1145.6 4.6 all-to-all-start.1
  1155.3 4.0 bitcast_dynamic-update-slice_fusion
  1159.3 13.3 %all-to-all-done.1 = bf16[16,32,8,256]{3,2,1,0:T(8,128)(2,1)} async-done(((bf16[16,32,8,256]{3,2,1,0:T(8,128)(2,1)}), bf16[16,32,8,256]{3,2,1,0:T(8,128)(2,1)}, u32[]{:S(2)}, u32[]{:S(2)}) %all-to-all-start.1) | async-done | bytes 2097184 | tf_op jit(solution)/shard_map/all_to_all | solution.py:22
  (234 shorter events, 142.1 us)
Async XLA Ops:
  0.6 21.1 %copy-start = (bf16[1,16,8,4096]{3,2,1,0:T(8,128)(2,1)S(1)}, bf16[1,16,8,4096]{3,2,1,0:T(8,128)(2,1)}, u32[]{:S(2)}) copy-start(bf16[1,16,8,4096]{3,2,1,0:T(8,128)(2,1)} %param.24) | copy-start | bytes 3145732
  12.9 8.4 copy-start.22
  12.9 8.6 copy-start.18
  12.9 510.1 %all-to-all-start = ((bf16[16,256,4096]{2,1,0:T(8,128)(2,1)}), bf16[16,256,4096]{2,1,0:T(8,128)(2,1)}, u32[]{:S(2)}, u32[]{:S(2)}) async-start(bf16[16,256,4096]{2,1,0:T(8,128)(2,1)} %stack.3), calls=%async_computation | async-start | bytes 67108864 | tf_op jit(solution)/shard_map/all_to_all | solution.py:89
  21.2 2.2 copy-start.16
  21.2 4.5 copy-start.23
  21.7 8.0 copy-start.21
  23.3 6.4 copy-start.10
  25.0 4.7 copy-start.13
  523.2 2.7 copy-start.9
  550.9 4.1 collective-permute-start
  555.0 1.0 copy-start.7
  581.0 5.1 collective-permute-start
  586.1 1.0 copy-start.7
  591.1 34.9 %collective-permute-start = (bf16[128,4096]{1,0:T(8,128)(2,1)}, bf16[128,4096]{1,0:T(8,128)(2,1)S(1)}, u32[]{:S(2)}, u32[]{:S(2)}) collective-permute-start(bf16[128,4096]{1,0:T(8,128)(2,1)} %get-tuple-element.1159), channel_id=1, source_target_pairs={{0,16},{16,32},{32,48},{48,64},{64,80},{80,96},{96,112},{1,17},{17... | collective-permute-start | bytes 3145736 | tf_op jit(solution)/shard_map/while/body/eval_jaxpr/ppermute | solution.py:12
  626.0 1.0 copy-start.7
  631.1 16.6 %collective-permute-start = (bf16[128,4096]{1,0:T(8,128)(2,1)}, bf16[128,4096]{1,0:T(8,128)(2,1)S(1)}, u32[]{:S(2)}, u32[]{:S(2)}) collective-permute-start(bf16[128,4096]{1,0:T(8,128)(2,1)} %get-tuple-element.1159), channel_id=1, source_target_pairs={{0,16},{16,32},{32,48},{48,64},{64,80},{80,96},{96,112},{1,17},{17... | collective-permute-start | bytes 3145736 | tf_op jit(solution)/shard_map/while/body/eval_jaxpr/ppermute | solution.py:12
  647.7 1.0 copy-start.7
  652.7 37.5 %collective-permute-start = (bf16[128,4096]{1,0:T(8,128)(2,1)}, bf16[128,4096]{1,0:T(8,128)(2,1)S(1)}, u32[]{:S(2)}, u32[]{:S(2)}) collective-permute-start(bf16[128,4096]{1,0:T(8,128)(2,1)} %get-tuple-element.1159), channel_id=1, source_target_pairs={{0,16},{16,32},{32,48},{48,64},{64,80},{80,96},{96,112},{1,17},{17... | collective-permute-start | bytes 3145736 | tf_op jit(solution)/shard_map/while/body/eval_jaxpr/ppermute | solution.py:12
  690.3 1.0 copy-start.7
  695.3 16.6 %collective-permute-start = (bf16[128,4096]{1,0:T(8,128)(2,1)}, bf16[128,4096]{1,0:T(8,128)(2,1)S(1)}, u32[]{:S(2)}, u32[]{:S(2)}) collective-permute-start(bf16[128,4096]{1,0:T(8,128)(2,1)} %get-tuple-element.1159), channel_id=1, source_target_pairs={{0,16},{16,32},{32,48},{48,64},{64,80},{80,96},{96,112},{1,17},{17... | collective-permute-start | bytes 3145736 | tf_op jit(solution)/shard_map/while/body/eval_jaxpr/ppermute | solution.py:12
  712.0 1.0 copy-start.7
  717.0 16.6 %collective-permute-start = (bf16[128,4096]{1,0:T(8,128)(2,1)}, bf16[128,4096]{1,0:T(8,128)(2,1)S(1)}, u32[]{:S(2)}, u32[]{:S(2)}) collective-permute-start(bf16[128,4096]{1,0:T(8,128)(2,1)} %get-tuple-element.1159), channel_id=1, source_target_pairs={{0,16},{16,32},{32,48},{48,64},{64,80},{80,96},{96,112},{1,17},{17... | collective-permute-start | bytes 3145736 | tf_op jit(solution)/shard_map/while/body/eval_jaxpr/ppermute | solution.py:12
  733.7 1.0 copy-start.7
  738.7 16.6 %collective-permute-start = (bf16[128,4096]{1,0:T(8,128)(2,1)}, bf16[128,4096]{1,0:T(8,128)(2,1)S(1)}, u32[]{:S(2)}, u32[]{:S(2)}) collective-permute-start(bf16[128,4096]{1,0:T(8,128)(2,1)} %get-tuple-element.1159), channel_id=1, source_target_pairs={{0,16},{16,32},{32,48},{48,64},{64,80},{80,96},{96,112},{1,17},{17... | collective-permute-start | bytes 3145736 | tf_op jit(solution)/shard_map/while/body/eval_jaxpr/ppermute | solution.py:12
  755.3 1.0 copy-start.7
  764.0 32.4 %collective-permute-start.1 = (bf16[128,4096]{1,0:T(8,128)(2,1)}, bf16[128,4096]{1,0:T(8,128)(2,1)S(1)}, u32[]{:S(2)}, u32[]{:S(2)}) collective-permute-start(bf16[128,4096]{1,0:T(8,128)(2,1)} %get-tuple-element.1176), channel_id=1, source_target_pairs={{16,0},{32,16},{48,32},{64,48},{80,64},{96,80},{112,96},{17,1},{33... | collective-permute-start | bytes 3145736 | tf_op jit(solution)/shard_map/while/body/eval_jaxpr/ppermute | solution.py:12
  765.3 3.3 copy-start.2
  771.4 25.1 %copy-start.3 = (f32[16,8,4096]{2,1,0:T(8,128)}, f32[16,8,4096]{2,1,0:T(8,128)S(1)}, u32[]{:S(2)}) copy-start(f32[16,8,4096]{2,1,0:T(8,128)S(1)} %get-tuple-element.1273) | copy-start | bytes 6291460 | tf_op jit(solution)/shard_map/while
  796.5 1.0 copy-start.6
  799.7 17.0 %collective-permute-start.1 = (bf16[128,4096]{1,0:T(8,128)(2,1)}, bf16[128,4096]{1,0:T(8,128)(2,1)S(1)}, u32[]{:S(2)}, u32[]{:S(2)}) collective-permute-start(bf16[128,4096]{1,0:T(8,128)(2,1)} %get-tuple-element.1176), channel_id=1, source_target_pairs={{16,0},{32,16},{48,32},{64,48},{80,64},{96,80},{112,96},{17,1},{33... | collective-permute-start | bytes 3145736 | tf_op jit(solution)/shard_map/while/body/eval_jaxpr/ppermute | solution.py:12
  801.0 3.3 copy-start.2
  808.6 8.1 copy-start.3
  819.9 16.3 %collective-permute-start.1 = (bf16[128,4096]{1,0:T(8,128)(2,1)}, bf16[128,4096]{1,0:T(8,128)(2,1)S(1)}, u32[]{:S(2)}, u32[]{:S(2)}) collective-permute-start(bf16[128,4096]{1,0:T(8,128)(2,1)} %get-tuple-element.1176), channel_id=1, source_target_pairs={{16,0},{32,16},{48,32},{64,48},{80,64},{96,80},{112,96},{17,1},{33... | collective-permute-start | bytes 3145736 | tf_op jit(solution)/shard_map/while/body/eval_jaxpr/ppermute | solution.py:12
  821.2 3.3 copy-start.2
  828.8 7.4 copy-start.3
  836.2 1.0 copy-start.6
  839.4 16.8 %collective-permute-start.1 = (bf16[128,4096]{1,0:T(8,128)(2,1)}, bf16[128,4096]{1,0:T(8,128)(2,1)S(1)}, u32[]{:S(2)}, u32[]{:S(2)}) collective-permute-start(bf16[128,4096]{1,0:T(8,128)(2,1)} %get-tuple-element.1176), channel_id=1, source_target_pairs={{16,0},{32,16},{48,32},{64,48},{80,64},{96,80},{112,96},{17,1},{33... | collective-permute-start | bytes 3145736 | tf_op jit(solution)/shard_map/while/body/eval_jaxpr/ppermute | solution.py:12
  840.7 3.3 copy-start.2
  848.3 7.9 copy-start.3
  856.2 1.0 copy-start.6
  859.4 32.2 %collective-permute-start.1 = (bf16[128,4096]{1,0:T(8,128)(2,1)}, bf16[128,4096]{1,0:T(8,128)(2,1)S(1)}, u32[]{:S(2)}, u32[]{:S(2)}) collective-permute-start(bf16[128,4096]{1,0:T(8,128)(2,1)} %get-tuple-element.1176), channel_id=1, source_target_pairs={{16,0},{32,16},{48,32},{64,48},{80,64},{96,80},{112,96},{17,1},{33... | collective-permute-start | bytes 3145736 | tf_op jit(solution)/shard_map/while/body/eval_jaxpr/ppermute | solution.py:12
  860.7 3.3 copy-start.2
  868.3 23.3 %copy-start.3 = (f32[16,8,4096]{2,1,0:T(8,128)}, f32[16,8,4096]{2,1,0:T(8,128)S(1)}, u32[]{:S(2)}) copy-start(f32[16,8,4096]{2,1,0:T(8,128)S(1)} %get-tuple-element.1273) | copy-start | bytes 6291460 | tf_op jit(solution)/shard_map/while
  894.8 17.0 %collective-permute-start.1 = (bf16[128,4096]{1,0:T(8,128)(2,1)}, bf16[128,4096]{1,0:T(8,128)(2,1)S(1)}, u32[]{:S(2)}, u32[]{:S(2)}) collective-permute-start(bf16[128,4096]{1,0:T(8,128)(2,1)} %get-tuple-element.1176), channel_id=1, source_target_pairs={{16,0},{32,16},{48,32},{64,48},{80,64},{96,80},{112,96},{17,1},{33... | collective-permute-start | bytes 3145736 | tf_op jit(solution)/shard_map/while/body/eval_jaxpr/ppermute | solution.py:12
  896.1 3.3 copy-start.2
  903.7 8.1 copy-start.3
  915.0 157.1 %collective-permute-start.1 = (bf16[128,4096]{1,0:T(8,128)(2,1)}, bf16[128,4096]{1,0:T(8,128)(2,1)S(1)}, u32[]{:S(2)}, u32[]{:S(2)}) collective-permute-start(bf16[128,4096]{1,0:T(8,128)(2,1)} %get-tuple-element.1176), channel_id=1, source_target_pairs={{16,0},{32,16},{48,32},{64,48},{80,64},{96,80},{112,96},{17,1},{33... | collective-permute-start | bytes 3145736 | tf_op jit(solution)/shard_map/while/body/eval_jaxpr/ppermute | solution.py:12
  916.3 3.3 copy-start.2
  923.9 148.1 %copy-start.3 = (f32[16,8,4096]{2,1,0:T(8,128)}, f32[16,8,4096]{2,1,0:T(8,128)S(1)}, u32[]{:S(2)}) copy-start(f32[16,8,4096]{2,1,0:T(8,128)S(1)} %get-tuple-element.1273) | copy-start | bytes 6291460 | tf_op jit(solution)/shard_map/while
  1076.0 16.0 %copy-start.17 = (bf16[128,8]{0,1:T(8,128)(2,1)}, bf16[128,8]{0,1:T(8,128)(2,1)S(1)}, u32[]{:S(2)}) copy-start(bf16[128,8]{0,1:T(8,128)(2,1)S(1)} %convolution_convert_fusion.1) | copy-start | bytes 6148 | tf_op jit(solution)/shard_map/while/body/eval_jaxpr/cond
  1092.8 4.1 copy-start.19
  1098.9 16.3 %collective-permute-start.1 = (bf16[128,4096]{1,0:T(8,128)(2,1)}, bf16[128,4096]{1,0:T(8,128)(2,1)S(1)}, u32[]{:S(2)}, u32[]{:S(2)}) collective-permute-start(bf16[128,4096]{1,0:T(8,128)(2,1)} %get-tuple-element.1176), channel_id=1, source_target_pairs={{16,0},{32,16},{48,32},{64,48},{80,64},{96,80},{112,96},{17,1},{33... | collective-permute-start | bytes 3145736 | tf_op jit(solution)/shard_map/while/body/eval_jaxpr/ppermute | solution.py:12
  1100.2 3.6 copy-start.2
  1108.1 7.1 copy-start.3
  1116.2 1.7 copy-start.15
  1118.4 16.0 %copy-start.12 = (bf16[2,8,4096]{2,0,1:T(2,128)(2,1)S(1)}, bf16[2,8,4096]{2,0,1:T(2,128)(2,1)}, u32[]{:S(2)}) copy-start(bf16[2,8,4096]{2,0,1:T(2,128)(2,1)} %get-tuple-element.936) | copy-start | bytes 393220 | tf_op jit(solution)/shard_map/cond
  1145.6 4.6 copy-start.4
  1145.6 27.0 %all-to-all-start.1 = ((bf16[16,32,8,256]{3,2,1,0:T(8,128)(2,1)}), bf16[16,32,8,256]{3,2,1,0:T(8,128)(2,1)}, u32[]{:S(2)}, u32[]{:S(2)}) async-start(bf16[16,32,8,256]{3,2,1,0:T(8,128)(2,1)} %copy.43), calls=%async_computation.1 | async-start | bytes 4194304 | tf_op jit(solution)/shard_map/all_to_all | solution.py:22
  1150.2 2.3 copy-start.5
  1150.2 2.6 copy-start.8
  1150.2 2.6 copy-start.11
  1150.3 2.6 copy-start.14
  1155.3 19.9 %copy-start.1 = (bf16[1,16,8,4096]{3,2,1,0:T(8,128)(2,1)S(1)}, bf16[1,16,8,4096]{3,2,1,0:T(8,128)(2,1)}, u32[]{:S(2)}) copy-start(bf16[1,16,8,4096]{3,2,1,0:T(8,128)(2,1)} %param.24) | copy-start | bytes 3145732
  (5 other events, 5.0 us)
